TPU v7x, 512 devices: a whole 4x4x16 slice. The times are simulated.
512 devices in a mesh: gx: 8 (over z_hi, x), gy: 32 (over z_lo, y), gz: 2 (over core).
Axes of the slice: x: 4, y: 4, z: 16 (z_hi: 2, z_lo: 8; z = z_hi * 8 + z_lo), core: 2. Of those that a mesh axis runs over, the one named last changes fastest.
Arguments:
- fields: float32 [2, 16, 2048, 2048], P(None, 'gz', 'gy', 'gx'), may hold values from -6 to 6
- factor: float32 [2048, 128], replicated, may hold values from -0.125 to 0.125
Outputs:
- gram: float32 [2048, 2048], P('gy', ('gx', 'gz'))
All inputs are finite; a program needn't handle non-finite values.
Results may differ from a plain program's by a relative error of at most 0.000054.
Values sent between devices are 32-bit elements; how exact they have to be, the bound alone decides.
A program may use at most 64 MiB of HBM per device.

v0:
```python
import jax
import jax.numpy as jnp
from jax import lax
from jax.experimental import pallas as pl
from jax.experimental.pallas import tpu as pltpu
from jax.sharding import PartitionSpec as P

MESH = pl.DeviceIdType.MESH
HIGHEST = lax.Precision.HIGHEST
NT = (((1,), (1,)), ((), ()))

XRS, ZHI, HALO, RZ, CA, RY, CY, PER = 0, 3, 4, 8, 11, 12, 16, 18
GRS, FIN, COPIES = 2 * PER, 2 * PER + 14, 2 * PER + 18


def smooth(p, length):
    return (
        p[0:length] + 4.0 * p[1 : length + 1] + 6.0 * p[2 : length + 2]
        + 4.0 * p[3 : length + 3] + p[4 : length + 4]
    ) * 0.0625


def beside(u):
    half = u.shape[0] // 2
    return jnp.concatenate([u[0:half], u[half:]], axis=1)


def kernel(
    f_ref, fac_ref, o_ref,
    fbuf, fac, sf, part, xin, tsum, zin, hin, rbuf, cbuf, gacc, gsend, gin, wsend, win,
    fsem, ssem, rsem, lsem,
):
    gx, gy, k = lax.axis_index("gx"), lax.axis_index("gy"), lax.axis_index("gz")
    h, x = gx // 4, gx % 4
    zlo, y = gy // 4, gy % 4
    a, m = zlo // 4, zlo % 4
    ye, yd = y + 1 - 2 * (y % 2), 3 - y

    def dev(h=h, x=x, a=a, m=m, y=y, k=k):
        return (h * 4 + x, (a * 4 + m) * 4 + y, k)

    x_peers = [(x + d) % 4 for d in range(1, 4)]
    m_peers = [(m + d) % 4 for d in range(1, 4)]
    g_peers = [((x + dx) % 4, (k + dk) % 2) for dx in range(4) for dk in range(2) if dx + dk]
    up, down = (gy + 1) % 32, (gy + 31) % 32
    fin_self = x == m

    lo = pl.multiple_of(jnp.maximum(gx * 256 - 8, 0), 8)
    mid = pl.multiple_of(gx * 256, 8)
    hi = pl.multiple_of(jnp.minimum(gx * 256 + 256, 2040), 8)
    loads = [
        pltpu.make_async_copy(fac_ref.at[pl.ds(lo, 8)], fac.at[pl.ds(0, 8)], fsem.at[0]),
        pltpu.make_async_copy(fac_ref.at[pl.ds(mid, 256)], fac.at[pl.ds(8, 256)], fsem.at[1]),
        pltpu.make_async_copy(fac_ref.at[pl.ds(hi, 8)], fac.at[pl.ds(264, 8)], fsem.at[2]),
    ]
    order = (2, 1, 3, 0)
    fields = {}
    for v in range(2):
        for i in range(4):
            xp = (x + order[i]) % 4
            fields[v, i] = pltpu.make_async_copy(
                f_ref.at[v, pl.ds(2 * xp, 2)], fbuf.at[v, i], fsem.at[3 + 4 * v + i]
            )
    for c in loads + list(fields.values()):
        c.start()

    barrier = pltpu.get_barrier_semaphore()

    def greet(d):
        pl.semaphore_signal(barrier, inc=1, device_id=d, device_id_type=MESH)

    for rel in (1, 0):
        hq = (h + rel) % 2
        greet((hq * 4 + x, up, k))
        greet((hq * 4 + x, down, k))
        greet(dev(h=hq, x=m, m=x, y=ye))
    greet(dev(h=1 - h, x=m, m=x))
    greet(dev(h=1 - h))
    greet(dev(a=1 - a))
    for mp in m_peers:
        greet(dev(m=mp))
    for xp, kp in g_peers:
        greet(dev(x=xp, k=kp))
    greet(dev(y=ye))
    greet(dev(y=yd))

    @pl.when(jnp.logical_not(fin_self))
    def _():
        greet(dev(x=m, m=x))

    for c in loads:
        c.wait()
    before = jnp.where(gx > 0, fac[6:8, :], 0.0)
    after = jnp.where(gx < 7, fac[264:266, :], 0.0)
    sf[...] = smooth(jnp.concatenate([before, fac[8:264, :], after], axis=0), 256)

    sends = []

    def send(src, dst, number, device):
        c = pltpu.make_async_remote_copy(
            src_ref=src, dst_ref=dst, send_sem=ssem.at[number], recv_sem=rsem.at[number],
            device_id=device, device_id_type=MESH,
        )
        c.start()
        sends.append(c)
        return c

    def project(v, i):
        fields[v, i].wait()
        part[v, i] = jnp.dot(
            fbuf[v, i].reshape(128, 256), sf[...],
            precision=HIGHEST, preferred_element_type=jnp.float32,
        ).reshape(2, 64, 128)

    xrs = [[], []]
    for v in range(2):
        for i in range(3):
            d = order[i]
            project(v, i)
            if v == 0 and i == 0:
                pl.semaphore_wait(barrier, jnp.where(fin_self, 21, 22))
            xrs[v].append(send(part.at[v, i], xin.at[v, i], PER * v + XRS + i, dev(x=x_peers[d - 1])))
        project(v, 3)

    zhi = [[], []]
    for v in range(2):
        for c in xrs[v]:
            c.wait_recv()
        tsum[v] = part[v, 3] + xin[v, 0] + xin[v, 1] + xin[v, 2]
        zhi[v].append(send(tsum.at[v, 1 - h], zin.at[v], PER * v + ZHI, dev(h=1 - h)))
        for rel in (1, 0):
            hq = (h + rel) % 2
            number = PER * v + HALO + rel
            zhi[v].append(
                send(tsum.at[v, hq, pl.ds(0, 8)], hin.at[v, 1, rel], number + 2, (hq * 4 + x, down, k))
            )
            zhi[v].append(
                send(tsum.at[v, hq, pl.ds(56, 8)], hin.at[v, 0, rel], number, (hq * 4 + x, up, k))
            )

    zs, far, ys = [[], []], [], [[], []]
    for v in range(2):
        base = PER * v
        for c in zhi[v]:
            c.wait_recv()
        before = jnp.where(gy > 0, hin[v, 0, 0, 6:8] + hin[v, 0, 1, 6:8], 0.0)
        after = jnp.where(gy < 31, hin[v, 1, 0, 0:2] + hin[v, 1, 1, 0:2], 0.0)
        own = tsum[v, h] + zin[v]
        block = smooth(jnp.concatenate([before, own, after], axis=0), 64)
        rbuf[v, 0, m] = block
        cbuf[v, a, 0] = block
        mine = rbuf.at[v, 0, m]
        far.append(send(mine, cbuf.at[v, a, 0], base + CA, dev(a=1 - a)))
        for d in range(3):
            zs[v].append(send(mine, rbuf.at[v, 0, m], base + RZ + d, dev(m=m_peers[d])))
        ys[v].append(send(mine, rbuf.at[v, 1, m], base + RY, dev(y=ye)))
        ys[v].append(send(mine, cbuf.at[v, a, 1], base + CY, dev(y=yd)))
    for v in range(2):
        base = PER * v
        for d in (0, 2, 1):
            zs[v][d].wait_recv()
            src = (m + 3 - d) % 4
            ys[v].append(send(rbuf.at[v, 0, src], rbuf.at[v, 1, src], base + RY + 1 + d, dev(y=ye)))
        far[v].wait_recv()
        ys[v].append(send(cbuf.at[v, 1 - a, 0], cbuf.at[v, 1 - a, 1], base + CY + 1, dev(y=yd)))

    def tile(v, mp, kp):
        jd = jnp.where(y // 2 == kp, 0, 1)
        rows = jnp.concatenate([rbuf[v, 0, mp], rbuf[v, 1, mp]], axis=0)
        cols = jnp.concatenate([cbuf[v, h, jd], cbuf[v, 1 - h, jd]], axis=0)
        return lax.dot_general(
            rows, cols, NT, precision=HIGHEST, preferred_element_type=jnp.float32
        )

    turn = (3, 4, 1, 2, 5, 6, 0)
    for c in ys[0]:
        c.wait_recv()
    for i in turn:
        gacc[i] = tile(0, *g_peers[i])
    gacc[7] = tile(0, x, k)
    for c in ys[1]:
        c.wait_recv()

    grs = [[], []]
    for i in turn:
        xp, kp = g_peers[i]
        t = gacc[i] + tile(1, xp, kp)
        gsend[1, i] = beside(t[:, 64:128])
        grs[1].append(send(gsend.at[1, i], gin.at[1, i], GRS + 7 + i, dev(x=xp, k=kp)))
        gsend[0, i] = beside(t[:, 0:64])
    for i in turn:
        xp, kp = g_peers[i]
        grs[0].append(send(gsend.at[0, i], gin.at[0, i], GRS + i, dev(x=xp, k=kp)))
    t = gacc[7] + tile(1, x, k)

    fin = []
    for rel in (1, 0):
        for c in grs[rel]:
            c.wait_recv()
        total = beside(t[:, 64 * rel : 64 * rel + 64])
        for i in range(7):
            total = total + gin[rel, i]
        aq = (h + rel) % 2
        for j in (1, 0):
            wsend[rel, j] = beside(total[:, j * 64 : (j + 1) * 64])
            target = dev(h=aq, x=m, m=x, y=ye if j else y)
            number = FIN + 2 * rel + j
            if rel or j:
                fin.append(send(wsend.at[rel, j], win.at[rel, j], number, target))
            else:
                own = pltpu.make_async_copy(wsend.at[0, 0], win.at[0, 0], lsem)

                @pl.when(fin_self)
                def _():
                    own.start()
                    own.wait()

                @pl.when(jnp.logical_not(fin_self))
                def _():
                    c = pltpu.make_async_remote_copy(
                        src_ref=wsend.at[0, 0], dst_ref=win.at[0, 0],
                        send_sem=ssem.at[number], recv_sem=rsem.at[number],
                        device_id=target, device_id_type=MESH,
                    )
                    c.start()
                    c.wait()

    for c in fin:
        c.wait_recv()
    blocks = []
    for j in range(2):
        w = (win[0, j] + win[1, j]) * (1.0 / 64.0)
        blocks.append(jnp.concatenate([w[:, 0:64], w[:, 64:128]], axis=0))
    first = jnp.where(y // 2 == k, y % 2, 1 - y % 2)
    o_ref[...] = jnp.where(
        first == 0,
        jnp.concatenate(blocks, axis=1),
        jnp.concatenate(blocks[::-1], axis=1),
    )
    for c in sends:
        c.wait_send()


def local(fields, factor):
    f32 = jnp.float32
    hbm = pl.BlockSpec(memory_space=pltpu.HBM)
    return pl.pallas_call(
        kernel,
        out_shape=jax.ShapeDtypeStruct((64, 128), f32),
        in_specs=[hbm, hbm],
        out_specs=pl.BlockSpec(memory_space=pltpu.VMEM),
        scratch_shapes=[
            pltpu.VMEM((2, 4, 2, 64, 256), f32),
            pltpu.VMEM((272, 128), f32),
            pltpu.VMEM((256, 128), f32),
            pltpu.VMEM((2, 4, 2, 64, 128), f32),
            pltpu.VMEM((2, 3, 2, 64, 128), f32),
            pltpu.VMEM((2, 2, 64, 128), f32),
            pltpu.VMEM((2, 64, 128), f32),
            pltpu.VMEM((2, 2, 2, 8, 128), f32),
            pltpu.VMEM((2, 2, 4, 64, 128), f32),
            pltpu.VMEM((2, 2, 2, 64, 128), f32),
            pltpu.VMEM((8, 128, 128), f32),
            pltpu.VMEM((2, 7, 64, 128), f32),
            pltpu.VMEM((2, 7, 64, 128), f32),
            pltpu.VMEM((2, 2, 32, 128), f32),
            pltpu.VMEM((2, 2, 32, 128), f32),
            pltpu.SemaphoreType.DMA((11,)),
            pltpu.SemaphoreType.DMA((COPIES,)),
            pltpu.SemaphoreType.DMA((COPIES,)),
            pltpu.SemaphoreType.DMA,
        ],
        compiler_params=pltpu.CompilerParams(
            collective_id=0, has_side_effects=True, vmem_limit_bytes=48 << 20
        ),
        cost_estimate=pl.CostEstimate(flops=135_000_000, bytes_accessed=1_300_000, transcendentals=0),
    )(fields, factor)


def solution(mesh):
    in_specs = (P(None, "gz", "gy", "gx"), P())
    out_specs = P("gy", ("gx", "gz"))
    return jax.shard_map(local, mesh=mesh, in_specs=in_specs, out_specs=out_specs, check_vma=False)
```

profile of v0, /device:TPU:1, one launch (start us, length us, event | category | flops | bytes accessed | tf_op | source)
XLA Modules:
  0.0 67.2 jit_solution(8002136300136877295)
XLA Ops:
  0.0 0.0 copy-start
  0.0 1.2 %copy-done = f32[2,8,64,256]{3,2,1,0:T(8,128)S(1)} copy-done((f32[2,8,64,256]{3,2,1,0:T(8,128)S(1)}, f32[2,8,64,256]{3,2,1,0:T(8,128)}, u32[]{:S(2)}) %copy-start) | copy-done | bytes 1048600
  1.2 0.0 copy-start.1
  1.2 1.2 %copy-done.1 = f32[2048,128]{1,0:T(8,128)S(1)} copy-done((f32[2048,128]{1,0:T(8,128)S(1)}, f32[2048,128]{1,0:T(8,128)}, u32[]{:S(2)}) %copy-start.1) | copy-done | bytes 1048600
  2.5 64.2 %shard_map.28 = f32[64,128]{1,0:T(8,128)S(1)} custom-call(f32[2,8,64,256]{3,2,1,0:T(8,128)S(1)} %copy-done, f32[2048,128]{1,0:T(8,128)S(1)} %copy-done.1), custom_call_target="tpu_custom_call" | custom-call | flops 135000000 | bytes 1300000 | tf_op jit(solution)/shard_map/pallas_call | solution.py:247
  66.6 0.6 copy.4
Async XLA Ops:
  0.0 1.2 %copy-start = (f32[2,8,64,256]{3,2,1,0:T(8,128)S(1)}, f32[2,8,64,256]{3,2,1,0:T(8,128)}, u32[]{:S(2)}) copy-start(f32[2,8,64,256]{3,2,1,0:T(8,128)} %f_ref.1) | copy-start | bytes 3145732
  1.2 1.2 %copy-start.1 = (f32[2048,128]{1,0:T(8,128)S(1)}, f32[2048,128]{1,0:T(8,128)}, u32[]{:S(2)}) copy-start(f32[2048,128]{1,0:T(8,128)} %fac_ref.1) | copy-start | bytes 3145732
where the time goes:
time: 68.3 us; the launch traced here: 67.2 us
  Pallas kernels  64.2 us (94%)
  local copies, waits for them, and re-layouts  3.07 us (4%)
    pallas_call x1, Pallas kernels, local(): pl.pallas_call(kernel, out_shape=jax.ShapeDtypeStruct((64, 128), f32), in...  64.2 us
    unnamed x5, local copies, waits for them, and re-layouts  3.07 us

commit v1 on v0

v1 whole, which is shorter than its diff:
```python
import jax
import jax.numpy as jnp
from jax import lax
from jax.experimental import pallas as pl
from jax.experimental.pallas import tpu as pltpu
from jax.sharding import PartitionSpec as P

MESH = pl.DeviceIdType.MESH
HIGHEST = lax.Precision.HIGHEST
NT = (((1,), (1,)), ((), ()))

XRS, ZHI, HALO, RZ, CA, RY, CY, PER = 0, 3, 4, 8, 11, 12, 16, 18
GRS, FIN, COPIES = 2 * PER, 2 * PER + 14, 2 * PER + 18


def smooth(p, length):
    return (
        p[0:length] + 4.0 * p[1 : length + 1] + 6.0 * p[2 : length + 2]
        + 4.0 * p[3 : length + 3] + p[4 : length + 4]
    ) * 0.0625


def beside(u):
    half = u.shape[0] // 2
    return jnp.concatenate([u[0:half], u[half:]], axis=1)


def kernel(
    f_ref, fac_ref, o_ref,
    fbuf, fac, sf, part, xin, tsum, zin, hin, rbuf, cbuf, gacc, gsend, gin, wsend, win,
    fsem, ssem, rsem, reply,
):
    gx, gy, k = lax.axis_index("gx"), lax.axis_index("gy"), lax.axis_index("gz")
    h, x = gx // 4, gx % 4
    zlo, y = gy // 4, gy % 4
    a, m = zlo // 4, zlo % 4
    ye, yd = y + 1 - 2 * (y % 2), 3 - y

    def dev(h=h, x=x, a=a, m=m, y=y, k=k):
        return (h * 4 + x, (a * 4 + m) * 4 + y, k)

    x_peers = [(x + d) % 4 for d in range(1, 4)]
    m_peers = [(m + d) % 4 for d in range(1, 4)]
    g_peers = [((x + dx) % 4, (k + dk) % 2) for dx in range(4) for dk in range(2) if dx + dk]
    up, down = (gy + 1) % 32, (gy + 31) % 32
    has_up, has_down = gy < 31, gy > 0
    sides = jnp.where(has_up, 1, 0) + jnp.where(has_down, 1, 0)

    lo = pl.multiple_of(jnp.maximum(gx * 256 - 8, 0), 8)
    mid = pl.multiple_of(gx * 256, 8)
    hi = pl.multiple_of(jnp.minimum(gx * 256 + 256, 2040), 8)
    loads = [
        pltpu.make_async_copy(fac_ref.at[pl.ds(lo, 8)], fac.at[pl.ds(0, 8)], fsem.at[0]),
        pltpu.make_async_copy(fac_ref.at[pl.ds(mid, 256)], fac.at[pl.ds(8, 256)], fsem.at[1]),
        pltpu.make_async_copy(fac_ref.at[pl.ds(hi, 8)], fac.at[pl.ds(264, 8)], fsem.at[2]),
    ]
    order = (2, 1, 3, 0)
    fields = {}
    for v in range(2):
        for i in range(4):
            xp = (x + order[i]) % 4
            fields[v, i] = pltpu.make_async_copy(
                f_ref.at[v, pl.ds(2 * xp, 2)], fbuf.at[v, i], fsem.at[3 + 4 * v + i]
            )
    for c in loads + list(fields.values()):
        c.start()

    hin[...] = jnp.zeros_like(hin)
    barrier = pltpu.get_barrier_semaphore()

    def greet(d, semaphore=barrier, when=None):
        def tell():
            pl.semaphore_signal(semaphore, inc=1, device_id=d, device_id_type=MESH)

        if when is None:
            tell()
        else:
            pl.when(when)(tell)

    greet(dev(h=1), when=h == 0)
    greet((4 + x, up, k), when=(h == 0) & has_up)
    greet((4 + x, down, k), when=(h == 0) & has_down)
    greet(dev(a=1), when=a == 0)
    for mp in m_peers:
        greet(dev(m=mp), when=mp > m)
    for xp, kp in g_peers:
        greet(dev(x=xp, k=kp))
    greet(dev(y=ye))
    greet(dev(y=yd))
    greet((gx, up, k), when=has_up)
    greet((gx, down, k), when=has_down)

    for c in loads:
        c.wait()
    before = jnp.where(gx > 0, fac[6:8, :], 0.0)
    after = jnp.where(gx < 7, fac[264:266, :], 0.0)
    sf[...] = smooth(jnp.concatenate([before, fac[8:264, :], after], axis=0), 256)

    sends = []

    def send(src, dst, number, device, when=None):
        c = pltpu.make_async_remote_copy(
            src_ref=src, dst_ref=dst, send_sem=ssem.at[number], recv_sem=rsem.at[number],
            device_id=device, device_id_type=MESH,
        )
        if when is None:
            c.start()
        else:
            pl.when(when)(c.start)
        sends.append((c, when))
        return c

    def project(v, i):
        fields[v, i].wait()
        part[v, i] = jnp.dot(
            fbuf[v, i].reshape(128, 256), sf[...],
            precision=HIGHEST, preferred_element_type=jnp.float32,
        ).reshape(2, 64, 128)

    xrs = [[], []]
    for v in range(2):
        for i in range(3):
            d = order[i]
            project(v, i)
            if v == 0 and i == 0:
                pl.semaphore_wait(barrier, 9 + sides + m + a + h * (1 + sides))
            xrs[v].append(send(part.at[v, i], xin.at[v, i], PER * v + XRS + i, dev(x=x_peers[d - 1])))
        if v == 0:
            for mp in m_peers:
                greet(dev(m=mp), reply, mp < m)
            greet(dev(a=0), reply, a == 1)
            greet(dev(h=0), reply, h == 1)
            greet((x, up, k), reply, (h == 1) & has_up)
            greet((x, down, k), reply, (h == 1) & has_down)
        project(v, 3)

    zhi, halos = [], [[], []]
    replies = 3 - m + 1 - a + (1 - h) * (1 + sides)
    for v in range(2):
        for c in xrs[v]:
            c.wait_recv()
        tsum[v] = part[v, 3] + xin[v, 0] + xin[v, 1] + xin[v, 2]
        if v == 0:

            @pl.when(replies > 0)
            def _():
                pl.semaphore_wait(reply, replies)

        zhi.append(send(tsum.at[v, 1 - h], zin.at[v], PER * v + ZHI, dev(h=1 - h)))
        for rel in (1, 0):
            hq = (h + rel) % 2
            number = PER * v + HALO + rel
            low = tsum.at[v, hq, pl.ds(0, 8)]
            c = send(low, hin.at[v, 1, rel], number + 2, (hq * 4 + x, down, k), has_down)
            halos[v].append((c, has_up))
            high = tsum.at[v, hq, pl.ds(56, 8)]
            c = send(high, hin.at[v, 0, rel], number, (hq * 4 + x, up, k), has_up)
            halos[v].append((c, has_down))

    zs, far, ys = [[], []], [], [[], []]
    for v in range(2):
        base = PER * v
        zhi[v].wait_recv()
        for c, when in halos[v]:
            pl.when(when)(c.wait_recv)
        before = hin[v, 0, 0, 6:8] + hin[v, 0, 1, 6:8]
        after = hin[v, 1, 0, 0:2] + hin[v, 1, 1, 0:2]
        own = tsum[v, h] + zin[v]
        block = smooth(jnp.concatenate([before, own, after], axis=0), 64)
        rbuf[v, 0, m] = block
        cbuf[v, a, 0] = block
        mine = rbuf.at[v, 0, m]
        for d in range(3):
            zs[v].append(send(mine, rbuf.at[v, 0, m], base + RZ + d, dev(m=m_peers[d])))
        ys[v].append(send(mine, rbuf.at[v, 1, m], base + RY, dev(y=ye)))
        ys[v].append(send(mine, cbuf.at[v, a, 1], base + CY, dev(y=yd)))
        far.append(send(mine, cbuf.at[v, a, 0], base + CA, dev(a=1 - a)))
    turned = []

    def turn_far(v):
        far[v].wait_recv()
        there = cbuf.at[v, 1 - a]
        turned.append(send(there.at[0], there.at[1], PER * v + CY + 1, dev(y=yd)))

    for v in range(2):
        base = PER * v
        for d in (0, 2, 1):
            zs[v][d].wait_recv()
            src = (m + 3 - d) % 4
            ys[v].append(send(rbuf.at[v, 0, src], rbuf.at[v, 1, src], base + RY + 1 + d, dev(y=ye)))
        if v == 0:
            turn_far(0)

    jd = jnp.where(y // 2 == k, 0, 1)

    def tile(v, mp, half):
        aq = 1 - a if half else a
        rows = jnp.concatenate([rbuf[v, 0, mp], rbuf[v, 1, mp]], axis=0)
        cols = jnp.concatenate([cbuf[v, aq, jd], cbuf[v, aq, 1 - jd]], axis=0)
        return lax.dot_general(
            rows, cols, NT, precision=HIGHEST, preferred_element_type=jnp.float32
        )

    def scatter(half):
        copies = []
        for dx in (2, 1, 3, 0):
            t = gacc[half, dx] + tile(1, (x + dx) % 4, half)
            for dk in (0, 1):
                i = 2 * dx - 1 + dk
                piece = beside(t[:, 64 * dk : 64 * dk + 64])
                if i < 0:
                    own = piece
                else:
                    xp, kp = g_peers[i]
                    gsend[half, i] = piece
                    number = GRS + 7 * half + i
                    copies.append(send(gsend.at[half, i], gin.at[half, i], number, dev(x=xp, k=kp)))
        return own, copies

    def deliver(half, own, copies):
        for c in copies:
            c.wait_recv()
        total = own
        for i in range(7):
            total = total + gin[half, i]
        aq = 1 - a if half else a
        rel = (h + aq) % 2
        for j in (1, 0):
            packed = beside(total[:, j * 64 : (j + 1) * 64])
            wsend[half, j] = packed
            target = dev(h=aq, x=m, m=x, y=ye if j else y)
            away = None if j else (x != m) | (rel != 0)
            send(wsend.at[half, j], win.at[rel, j], FIN + 2 * rel + j, target, away)
            if j == 0:

                @pl.when(jnp.logical_not(away))
                def _():
                    win[0, 0] = packed

    for c in ys[0]:
        c.wait_recv()
    for dx in range(4):
        gacc[0, dx] = tile(0, (x + dx) % 4, 0)
    for c in ys[1]:
        c.wait_recv()
    first_half = scatter(0)
    turn_far(1)
    turned[0].wait_recv()
    for dx in range(4):
        gacc[1, dx] = tile(0, (x + dx) % 4, 1)
    turned[1].wait_recv()
    second_half = scatter(1)
    deliver(0, *first_half)
    deliver(1, *second_half)

    for rel in range(2):
        for j in range(2):
            number = FIN + 2 * rel + j
            c = pltpu.make_async_remote_copy(
                src_ref=wsend.at[rel, j], dst_ref=win.at[rel, j],
                send_sem=ssem.at[number], recv_sem=rsem.at[number],
                device_id=dev(x=m, m=x, h=(h + rel) % 2, y=ye if j else y), device_id_type=MESH,
            )
            if rel or j:
                c.wait_recv()
            else:
                pl.when(x != m)(c.wait_recv)
    blocks = []
    for j in range(2):
        w = (win[0, j] + win[1, j]) * (1.0 / 64.0)
        blocks.append(jnp.concatenate([w[:, 0:64], w[:, 64:128]], axis=0))
    first = jnp.where(y // 2 == k, y % 2, 1 - y % 2)
    o_ref[...] = jnp.where(
        first == 0,
        jnp.concatenate(blocks, axis=1),
        jnp.concatenate(blocks[::-1], axis=1),
    )
    for c, when in sends:
        if when is None:
            c.wait_send()
        else:
            pl.when(when)(c.wait_send)


def local(fields, factor):
    f32 = jnp.float32
    hbm = pl.BlockSpec(memory_space=pltpu.HBM)
    return pl.pallas_call(
        kernel,
        out_shape=jax.ShapeDtypeStruct((64, 128), f32),
        in_specs=[hbm, hbm],
        out_specs=pl.BlockSpec(memory_space=pltpu.VMEM),
        scratch_shapes=[
            pltpu.VMEM((2, 4, 2, 64, 256), f32),
            pltpu.VMEM((272, 128), f32),
            pltpu.VMEM((256, 128), f32),
            pltpu.VMEM((2, 4, 2, 64, 128), f32),
            pltpu.VMEM((2, 3, 2, 64, 128), f32),
            pltpu.VMEM((2, 2, 64, 128), f32),
            pltpu.VMEM((2, 64, 128), f32),
            pltpu.VMEM((2, 2, 2, 8, 128), f32),
            pltpu.VMEM((2, 2, 4, 64, 128), f32),
            pltpu.VMEM((2, 2, 2, 64, 128), f32),
            pltpu.VMEM((2, 4, 128, 128), f32),
            pltpu.VMEM((2, 7, 64, 128), f32),
            pltpu.VMEM((2, 7, 64, 128), f32),
            pltpu.VMEM((2, 2, 32, 128), f32),
            pltpu.VMEM((2, 2, 32, 128), f32),
            pltpu.SemaphoreType.DMA((11,)),
            pltpu.SemaphoreType.DMA((COPIES,)),
            pltpu.SemaphoreType.DMA((COPIES,)),
            pltpu.SemaphoreType.REGULAR,
        ],
        compiler_params=pltpu.CompilerParams(
            collective_id=0, has_side_effects=True, vmem_limit_bytes=60 << 20
        ),
        cost_estimate=pl.CostEstimate(flops=135_000_000, bytes_accessed=1_300_000, transcendentals=0),
    )(fields, factor)


def solution(mesh):
    in_specs = (P(None, "gz", "gy", "gx"), P())
    out_specs = P("gy", ("gx", "gz"))
    return jax.shard_map(local, mesh=mesh, in_specs=in_specs, out_specs=out_specs, check_vma=False)
```

time: 68.3 us -> 63.1 us (0.924)
  the two profiles are of different devices: /device:TPU:1 before, /device:TPU:12 now
where the time goes in v1:
time: 63.1 us; the launch traced here: 62.9 us
  Pallas kernels  61.5 us (97%)
  local copies, waits for them, and re-layouts  1.38 us (2%)
    pallas_call x1, Pallas kernels, local(): pl.pallas_call(kernel, out_shape=jax.ShapeDtypeStruct((64, 128), f32), in...  61.5 us
    unnamed x1, local copies, waits for them, and re-layouts  1.38 us

profile of v1, /device:TPU:12, one launch (start us, length us, event | category | flops | bytes accessed | tf_op | source)
XLA Modules:
  0.0 62.9 jit_solution(665949372518045380)
XLA Ops:
  0.0 61.5 %shard_map.28 = f32[64,128]{1,0:T(8,128)} custom-call(f32[2,8,64,256]{3,2,1,0:T(8,128)} %f_ref.1, f32[2048,128]{1,0:T(8,128)} %fac_ref.1), custom_call_target="tpu_custom_call" | custom-call | flops 135000000 | bytes 1300000 | tf_op jit(solution)/shard_map/pallas_call | solution.py:288
  61.5 1.4 %copy.4 = f32[64,128]{1,0:T(8,128)} copy(f32[64,128]{1,0:T(8,128)} %shard_map.28) | data formatting | bytes 65536

commit v2 on v1

--- a/solution.py
+++ b/solution.py
@@ -146,7 +146,6 @@
             def _():
                 pl.semaphore_wait(reply, replies)
 
-        zhi.append(send(tsum.at[v, 1 - h], zin.at[v], PER * v + ZHI, dev(h=1 - h)))
         for rel in (1, 0):
             hq = (h + rel) % 2
             number = PER * v + HALO + rel
@@ -156,6 +155,7 @@
             high = tsum.at[v, hq, pl.ds(56, 8)]
             c = send(high, hin.at[v, 0, rel], number, (hq * 4 + x, up, k), has_up)
             halos[v].append((c, has_down))
+        zhi.append(send(tsum.at[v, 1 - h], zin.at[v], PER * v + ZHI, dev(h=1 - h)))
 
     zs, far, ys = [[], []], [], [[], []]
     for v in range(2):

time: 63.1 us -> 62.1 us (0.984)
  the two profiles are of different devices: /device:TPU:12 before, /device:TPU:4 now
where the time goes in v2:
time: 62.1 us; the launch traced here: 61.9 us
  Pallas kernels  60.5 us (97%)
  local copies, waits for them, and re-layouts  1.38 us (2%)
    pallas_call x1, Pallas kernels, local(): pl.pallas_call(kernel, out_shape=jax.ShapeDtypeStruct((64, 128), f32), in...  60.5 us
    unnamed x1, local copies, waits for them, and re-layouts  1.38 us

profile of v2, /device:TPU:4, one launch (start us, length us, event | category | flops | bytes accessed | tf_op | source)
XLA Modules:
  0.0 61.9 jit_solution(3889945982163331675)
XLA Ops:
  0.0 60.5 %shard_map.28 = f32[64,128]{1,0:T(8,128)} custom-call(f32[2,8,64,256]{3,2,1,0:T(8,128)} %f_ref.1, f32[2048,128]{1,0:T(8,128)} %fac_ref.1), custom_call_target="tpu_custom_call" | custom-call | flops 135000000 | bytes 1300000 | tf_op jit(solution)/shard_map/pallas_call | solution.py:288
  60.6 1.4 %copy.4 = f32[64,128]{1,0:T(8,128)} copy(f32[64,128]{1,0:T(8,128)} %shard_map.28) | data formatting | bytes 65536

commit v3 on v2

--- a/solution.py
+++ b/solution.py
@@ -241,13 +241,13 @@
         c.wait_recv()
     for dx in range(4):
         gacc[0, dx] = tile(0, (x + dx) % 4, 0)
+    turned[0].wait_recv()
+    for dx in range(4):
+        gacc[1, dx] = tile(0, (x + dx) % 4, 1)
     for c in ys[1]:
         c.wait_recv()
     first_half = scatter(0)
     turn_far(1)
-    turned[0].wait_recv()
-    for dx in range(4):
-        gacc[1, dx] = tile(0, (x + dx) % 4, 1)
     turned[1].wait_recv()
     second_half = scatter(1)
     deliver(0, *first_half)

time: 62.1 us -> 62.8 us (1.011)
  the two profiles are of different devices: /device:TPU:4 before, /device:TPU:6 now
where the time goes in v3:
time: 62.8 us; the launch traced here: 62.6 us
  Pallas kernels  61.2 us (97%)
  local copies, waits for them, and re-layouts  1.38 us (2%)
    pallas_call x1, Pallas kernels, local(): pl.pallas_call(kernel, out_shape=jax.ShapeDtypeStruct((64, 128), f32), in...  61.2 us
    unnamed x1, local copies, waits for them, and re-layouts  1.38 us

profile of v3, /device:TPU:6, one launch (start us, length us, event | category | flops | bytes accessed | tf_op | source)
XLA Modules:
  0.0 62.6 jit_solution(3720721088813198546)
XLA Ops:
  0.0 61.2 %shard_map.28 = f32[64,128]{1,0:T(8,128)} custom-call(f32[2,8,64,256]{3,2,1,0:T(8,128)} %f_ref.1, f32[2048,128]{1,0:T(8,128)} %fac_ref.1), custom_call_target="tpu_custom_call" | custom-call | flops 135000000 | bytes 1300000 | tf_op jit(solution)/shard_map/pallas_call | solution.py:288
  61.2 1.4 %copy.4 = f32[64,128]{1,0:T(8,128)} copy(f32[64,128]{1,0:T(8,128)} %shard_map.28) | data formatting | bytes 65536
